TPU v7x, 256 devices: a whole 4x4x8 slice. The times are simulated.
256 devices in a mesh: dp: 8 (over z), expert: 32 (over y, x, core).
Axes of the slice: x: 4, y: 4, z: 8, core: 2. Of those that a mesh axis runs over, the one named last changes fastest.
Arguments:
- activations: bfloat16 [32768, 4096], P(('dp', 'expert')), may hold values from -6 to 6
- out_grads: bfloat16 [32768, 2, 4096], P(('dp', 'expert')), may hold values from -6 to 6
- routes: int32 [32768, 2], P(('dp', 'expert')), may hold values from 0 to 7, as said below
Outputs:
- act_factor: float32 [32, 512, 4096], P('expert', 'dp')
- grad_factor: float32 [32, 512, 4096], P('expert', 'dp')
Inputs may be any that keep to these rules, and one draw needn't show every extreme that they name: `routes`: each row names 2 different experts. Among the 128 rows of one device no expert is named more than 48 times. One expert below 4, the same on every device, is named exactly 48 times by every device's rows, and on some device every expert below 4 is named exactly 48 times.
All inputs are finite; a program needn't handle non-finite values.
Results may differ from a plain program's by a relative error of at most 0.0003.
Values may be sent and summed in bfloat16 or wider, within the bound.
No kernel may reach another device: no remote copies, remote signals or barrier semaphores. Data moves between devices by JAX's collectives and lax.ppermute only.
A program may use at most 128 MiB of HBM per device.

v0:
```python
import jax
import jax.numpy as jnp
from jax import lax
from jax.sharding import PartitionSpec as P

EXPERTS = 8
TOP = 2
EXP_WIN = 4
CAP = 48


def on_device(activations, out_grads, routes):
    tok_rows = activations.shape[0]
    width = activations.shape[1]
    owners = lax.axis_size("expert")
    groups = lax.axis_size("dp")
    split = owners // EXP_WIN
    piece = width // split
    scale_norm = tok_rows * groups * owners * TOP / EXPERTS
    flat_routes = routes.reshape(TOP * tok_rows)
    hits = (flat_routes[:, None] == jnp.arange(EXP_WIN, dtype=jnp.int32)[None, :]).astype(jnp.int32)
    slots = jnp.cumsum(hits, axis=0) - hits
    placed = hits[:, :, None] * (
        slots[:, :, None] == jnp.arange(CAP, dtype=jnp.int32)[None, None, :]
    ).astype(jnp.int32)
    placed = (
        jnp.transpose(placed, (1, 2, 0)).reshape(EXP_WIN * CAP, TOP * tok_rows).astype(jnp.bfloat16)
    )
    token_placed = placed.reshape(EXP_WIN * CAP, tok_rows, TOP).sum(axis=-1)
    send_act = jnp.dot(token_placed, activations, preferred_element_type=jnp.float32).astype(
        jnp.bfloat16
    )
    send_grad = jnp.dot(
        placed, out_grads.reshape(TOP * tok_rows, width), preferred_element_type=jnp.float32
    ).astype(jnp.bfloat16)
    send_act = send_act.reshape(EXP_WIN, CAP, width)
    send_grad = send_grad.reshape(EXP_WIN, CAP, width)
    spread_act = jnp.broadcast_to(send_act[:, None], (EXP_WIN, split, CAP, width)).reshape(
        owners, CAP, width
    )
    spread_grad = jnp.broadcast_to(send_grad[:, None], (EXP_WIN, split, CAP, width)).reshape(
        owners, CAP, width
    )
    recv_act, recv_grad = (
        lax.all_to_all(spread_act, "expert", split_axis=0, concat_axis=0, tiled=True),
        lax.all_to_all(spread_grad, "expert", split_axis=0, concat_axis=0, tiled=True),
    )
    recv_act = recv_act.reshape(owners * CAP, width)
    recv_grad = recv_grad.reshape(owners * CAP, width)
    offset = lax.axis_index("expert") % split * piece
    rows_dev = piece // groups

    def gram_rows(data, count):
        columns = lax.dynamic_slice_in_dim(data, offset, count, 1)
        return lax.dot_general(
            columns, data, (((0,), (0,)), ((), ())), preferred_element_type=jnp.float32
        )

    summed = lax.psum_scatter(
        jnp.concatenate(
            [
                gram_rows(recv_act, lax.axis_size("dp") * rows_dev),
                gram_rows(recv_grad, lax.axis_size("dp") * rows_dev),
            ],
            axis=1,
        ),
        "dp",
        scatter_dimension=0,
        tiled=True,
    )
    act_block = summed[:, :width]
    grad_block = summed[:, width:]
    return ((act_block / scale_norm)[None], (grad_block / scale_norm)[None])


def solution(mesh):
    placed = (P(("dp", "expert"), None), P(("dp", "expert"), None, None), P(("dp", "expert"), None))
    return jax.shard_map(
        on_device,
        mesh=mesh,
        in_specs=placed,
        out_specs=(P("expert", "dp", None), P("expert", "dp", None)),
        check_vma=False,
    )
```

profile of v0, /device:TPU:4, one launch (start us, length us, event | category | flops | bytes accessed | tf_op | source)
XLA Modules:
  0.0 560.6 jit_solution(17979144844837652282)
XLA Ops:
  7.2 0.9 copy.19
  8.1 0.1 eq.70
  8.2 0.1 eq.66
  8.4 1.2 reduce-window.6
  9.6 0.1 slice.16
  9.7 0.1 copy.20
  9.8 0.1 copy.21
  9.9 0.1 add_bitcast_fusion
  10.0 2.7 reshape.111
  12.8 1.7 convolution_convert_fusion
  14.5 7.5 %broadcast_in_dim.27 = bf16[4,8,48,4096]{3,2,1,0:T(8,128)(2,1)} broadcast(bf16[4,48,4096]{2,1,0:T(8,128)(2,1)} %bitcast.28), dimensions={0,2,3} | broadcast | bytes 14155776 | tf_op jit(solution)/shard_map/broadcast_in_dim | solution.py:41
  22.0 7.6 %all-to-all-start.1 = ((bf16[32,48,4096]{2,1,0:T(8,128)(2,1)}), bf16[32,48,4096]{2,1,0:T(8,128)(2,1)}, u32[]{:S(2)}, u32[]{:S(2)}) async-start(bf16[32,48,4096]{2,1,0:T(8,128)(2,1)} %bitcast.27), calls=%async_computation.1 | async-start | bytes 25165824 | tf_op jit(solution)/shard_map/all_to_all | solution.py:46
  29.6 0.1 copy.25
  29.8 0.1 copy.27
  29.9 0.1 eq.77
  30.0 0.3 mul.15.clone
  30.4 0.4 mul.16
  30.8 0.3 eq.74.clone
  31.1 0.4 eq.75
  31.5 0.4 fusion.7
  32.0 0.6 convolution_convert_fusion.1
  32.6 147.2 %all-to-all-done.1 = bf16[32,48,4096]{2,1,0:T(8,128)(2,1)} async-done(((bf16[32,48,4096]{2,1,0:T(8,128)(2,1)}), bf16[32,48,4096]{2,1,0:T(8,128)(2,1)}, u32[]{:S(2)}, u32[]{:S(2)}) %all-to-all-start.1) | async-done | bytes 12582944 | tf_op jit(solution)/shard_map/all_to_all | solution.py:46
  179.8 6.2 %broadcast_in_dim.25 = bf16[4,8,48,4096]{3,2,1,0:T(8,128)(2,1)} broadcast(bf16[4,48,4096]{2,1,0:T(8,128)(2,1)S(1)} %bitcast.29), dimensions={0,2,3} | broadcast | bytes 14155776 | tf_op jit(solution)/shard_map/broadcast_in_dim | solution.py:38
  185.9 15.7 %all-to-all-start = ((bf16[32,48,4096]{2,1,0:T(8,128)(2,1)}), bf16[32,48,4096]{2,1,0:T(8,128)(2,1)}, u32[]{:S(2)}, u32[]{:S(2)}) async-start(bf16[32,48,4096]{2,1,0:T(8,128)(2,1)} %bitcast.26), calls=%async_computation | async-start | bytes 25165824 | tf_op jit(solution)/shard_map/all_to_all | solution.py:45
  201.6 0.2 reduce-scatter.2.cloned.1.call-start
  201.9 12.2 %fusion = f32[512,4096]{1,0:T(8,128)} fusion(bf16[1536,4096]{1,0:T(8,128)(2,1)} %bitcast.7, s32[]{:T(128)S(6)} %select_n.12), kind=kOutput, calls=%fused_computation.3 | convolution fusion | flops 6442450944 | bytes 22544388 | tf_op jit(solution)/shard_map/dot_general | solution.py:55
  214.1 137.5 %all-to-all-done = bf16[32,48,4096]{2,1,0:T(8,128)(2,1)} async-done(((bf16[32,48,4096]{2,1,0:T(8,128)(2,1)}), bf16[32,48,4096]{2,1,0:T(8,128)(2,1)}, u32[]{:S(2)}, u32[]{:S(2)}) %all-to-all-start) | async-done | bytes 12582944 | tf_op jit(solution)/shard_map/all_to_all | solution.py:45
  351.6 10.7 %fusion.2 = f32[512,4096]{1,0:T(8,128)S(1)} fusion(bf16[1536,4096]{1,0:T(8,128)(2,1)} %bitcast.3, s32[]{:T(128)S(6)} %select_n.12), kind=kOutput, calls=%fused_computation.5 | convolution fusion | flops 6442450944 | bytes 22544388 | tf_op jit(solution)/shard_map/dot_general | solution.py:55
  362.4 6.1 %pad_maximum_fusion = f32[512,8192]{1,0:T(8,128)} fusion(f32[512,4096]{1,0:T(8,128)S(1)} %copy-done.2, f32[512,4096]{1,0:T(8,128)S(1)} %fusion.2), kind=kLoop, calls=%fused_computation | loop fusion | flops 4194304 | bytes 33554432 | tf_op jit(solution)/shard_map/concatenate | solution.py:60
  368.5 0.0 reduce-scatter.2.cloned.1.call-update
  368.5 182.2 %reduce-scatter.2.cloned.1.call-done = f32[64,8192]{1,0:T(8,128)} async-done(((f32[512,8192]{1,0:T(8,128)}), f32[64,8192]{1,0:T(8,128)}) %reduce-scatter.2.cloned.1.call-update) | async-done | bytes 2097168 | tf_op jit(solution)/shard_map/reduce_scatter | solution.py:59
  550.7 3.0 fusion.4
  (13 shorter events, 0.1 us)
Async XLA Ops:
  7.2 24.8 %copy-start = (bf16[128,4096]{1,0:T(8,128)(2,1)S(1)}, bf16[128,4096]{1,0:T(8,128)(2,1)}, u32[]{:S(2)}) copy-start(bf16[128,4096]{1,0:T(8,128)(2,1)} %param.3) | copy-start | bytes 3145732
  22.0 157.8 %all-to-all-start.1 = ((bf16[32,48,4096]{2,1,0:T(8,128)(2,1)}), bf16[32,48,4096]{2,1,0:T(8,128)(2,1)}, u32[]{:S(2)}, u32[]{:S(2)}) async-start(bf16[32,48,4096]{2,1,0:T(8,128)(2,1)} %bitcast.27), calls=%async_computation.1 | async-start | bytes 25165824 | tf_op jit(solution)/shard_map/all_to_all | solution.py:46
  185.9 165.7 %all-to-all-start = ((bf16[32,48,4096]{2,1,0:T(8,128)(2,1)}), bf16[32,48,4096]{2,1,0:T(8,128)(2,1)}, u32[]{:S(2)}, u32[]{:S(2)}) async-start(bf16[32,48,4096]{2,1,0:T(8,128)(2,1)} %bitcast.26), calls=%async_computation | async-start | bytes 25165824 | tf_op jit(solution)/shard_map/all_to_all | solution.py:45
  201.6 349.1 %reduce-scatter.2.cloned.1.call-start = ((), (), s32[]{:S(2)}) async-start(), calls=%async_computation.3 | async-start | bytes 18874368 | tf_op jit(solution)/shard_map/reduce_scatter | solution.py:59
  351.6 10.7 %copy-start.2 = (f32[512,4096]{1,0:T(8,128)S(1)}, f32[512,4096]{1,0:T(8,128)}, u32[]{:S(2)}) copy-start(f32[512,4096]{1,0:T(8,128)} %fusion) | copy-start | bytes 25165828
  368.5 185.3 %copy-start.1 = (bf16[128,4096]{1,0:T(8,128)(2,1)S(1)}, bf16[128,4096]{1,0:T(8,128)(2,1)}, u32[]{:S(2)}) copy-start(bf16[128,4096]{1,0:T(8,128)(2,1)} %param.3) | copy-start | bytes 3145732
Sparse Core Ops, SparseCore 0:
  368.6 182.0 reduce-scatter.1
where the time goes:
time: 562 us; the launch traced here: 561 us
  waiting for transfers between devices  467 us (83%)
  matrix products  25.3 us (5%)
  starting transfers between devices  23.6 us (4%)
  local copies, waits for them, and re-layouts  19.7 us (4%)
  between operations  14.2 us (3%)
  other arithmetic  10.9 us (2%)
    reduce_scatter x1, waiting for transfers between devices, on_device(): lax.psum_scatter(jnp.concatenate([gram_rows(recv_act, lax.axis_size('dp')...  182 us
    all_to_all x1, waiting for transfers between devices, on_device(): lax.all_to_all(spread_grad, 'expert', split_axis=0, concat_axis=0, tiled=...  147 us
    all_to_all x1, waiting for transfers between devices, on_device(): lax.all_to_all(spread_act, 'expert', split_axis=0, concat_axis=0, tiled=T...  138 us
    dot_general x2, matrix products, gram_rows(): lax.dot_general(columns, data, (((0,), (0,)), ((), ())), preferred_elemen...  23 us
    all_to_all x1, starting transfers between devices, on_device(): lax.all_to_all(spread_act, 'expert', split_axis=0, concat_axis=0, tiled=T...  15.7 us
  transfers between devices with their start and end apart: 3, of which 3 were waited for; matrix products, arithmetic and copies ran while one was open for 3% of the time, Pallas kernels for 0%

commit v1 on v0

v1 whole, which is shorter than its diff:
```python
import jax
import jax.numpy as jnp
from jax import lax
from jax.experimental import pallas as pl
from jax.experimental.pallas import tpu as pltpu
from jax.sharding import Mesh, PartitionSpec as P

EXPERTS = 8
TOP = 2
EXP_WIN = 4
CAP = 48
TILE = 512


def shift(size, step):
    return [(i, (i + step) % size) for i in range(size)]


def gram_kernel(strip_ref, *refs):
    blocks = (len(refs) - 3) // 2
    left_refs, right_refs = refs[:blocks], refs[blocks : 2 * blocks]
    out_ref, left, right = refs[2 * blocks :]
    rows = left_refs[0].shape[0]

    @pl.when(pl.program_id(0) == 0)
    def _():
        for i, ref in enumerate(left_refs):
            left[i * rows : (i + 1) * rows, :] = ref[...]

    for i, ref in enumerate(right_refs):
        right[i * rows : (i + 1) * rows, :] = ref[...]
    out_ref[...] = lax.dot_general(
        left[...], right[...], (((0,), (0,)), ((), ())), preferred_element_type=jnp.float32
    ) * jnp.float32(1.0 / SCALE)


SCALE = 8192.0


def gram(strip, blocks, piece):
    rows, width = blocks[0].shape
    count = len(blocks)
    flops = 2 * count * rows * piece * width
    return pl.pallas_call(
        gram_kernel,
        out_shape=jax.ShapeDtypeStruct((piece, width), jnp.float32),
        grid_spec=pltpu.PrefetchScalarGridSpec(
            num_scalar_prefetch=1,
            grid=(width // TILE,),
            in_specs=[pl.BlockSpec((rows, piece), lambda j, s: (0, s[0]))] * count
            + [pl.BlockSpec((rows, TILE), lambda j, s: (0, j))] * count,
            out_specs=pl.BlockSpec((piece, TILE), lambda j, s: (0, j)),
            scratch_shapes=[
                pltpu.VMEM((count * rows, piece), jnp.bfloat16),
                pltpu.VMEM((count * rows, TILE), jnp.bfloat16),
            ],
        ),
        compiler_params=pltpu.CompilerParams(vmem_limit_bytes=40 * 2**20),
        cost_estimate=pl.CostEstimate(
            flops=flops, bytes_accessed=count * rows * width * 2 + piece * width * 4, transcendentals=0
        ),
    )(strip, *blocks, *blocks)


def ring_sum(part, groups):
    z = lax.axis_index("z")
    rows = part.shape[0] // groups
    half = rows // 2
    up, down = shift(groups, 1), shift(groups, -1)

    def chunk(step, first, count):
        at = lax.rem(z + step + groups, groups) * rows + first
        return lax.dynamic_slice_in_dim(part, at, count, 0)

    far = groups // 2
    from_low = lax.ppermute(chunk(far, 0, half), "z", up)
    from_high = lax.ppermute(chunk(-far, half, half), "z", down)
    for step in range(far - 1, 0, -1):
        own_up, own_down = chunk(step, 0, rows), chunk(-step, 0, rows)
        if step == far - 1:
            own_up = jnp.concatenate([own_up[:half] + from_low, own_up[half:]], axis=0)
            own_down = jnp.concatenate([own_down[:half], own_down[half:] + from_high], axis=0)
        else:
            own_up, own_down = own_up + from_low, own_down + from_high
        from_low = lax.ppermute(own_up, "z", up)
        from_high = lax.ppermute(own_down, "z", down)
    return chunk(0, 0, rows) + (from_low + from_high)


def spread(send):
    width = send.shape[-1]
    mine = lax.all_to_all(send, "y", split_axis=0, concat_axis=0, tiled=True)
    mine = mine.reshape(-1, width)
    chips = lax.axis_size("x")
    held = [mine] + [lax.ppermute(mine, "x", shift(chips, step)) for step in (1, chips - 1, 2)]
    return held + [lax.ppermute(block, "c", shift(2, 1)) for block in held]


def on_device(activations, out_grads, routes):
    tok_rows = activations.shape[0]
    width = activations.shape[1]
    groups = lax.axis_size("z")
    split = lax.axis_size("x") * lax.axis_size("c")
    piece = width // split
    flat_routes = routes.reshape(TOP * tok_rows)
    hits = (flat_routes[:, None] == jnp.arange(EXP_WIN, dtype=jnp.int32)[None, :]).astype(jnp.int32)
    slots = jnp.cumsum(hits, axis=0) - hits
    placed = hits[:, :, None] * (
        slots[:, :, None] == jnp.arange(CAP, dtype=jnp.int32)[None, None, :]
    ).astype(jnp.int32)
    placed = (
        jnp.transpose(placed, (1, 2, 0)).reshape(EXP_WIN * CAP, TOP * tok_rows).astype(jnp.bfloat16)
    )
    token_placed = placed.reshape(EXP_WIN * CAP, tok_rows, TOP).sum(axis=-1)
    send_act = jnp.dot(token_placed, activations, preferred_element_type=jnp.float32).astype(
        jnp.bfloat16
    )
    send_grad = jnp.dot(
        placed, out_grads.reshape(TOP * tok_rows, width), preferred_element_type=jnp.float32
    ).astype(jnp.bfloat16)
    strip = (lax.axis_index("x") * 2 + lax.axis_index("c")).astype(jnp.int32).reshape(1)
    act_rows = spread(send_act.reshape(EXP_WIN, CAP, width))
    act_part = gram(strip, act_rows, piece)
    act_block = lax.psum_scatter(act_part, "z", scatter_dimension=0, tiled=True)
    grad_rows = spread(send_grad.reshape(EXP_WIN, CAP, width))
    grad_part = gram(strip, grad_rows, piece)
    grad_block = ring_sum(grad_part, groups)
    return act_block[None], grad_block[None]


def solution(mesh):
    axes = ("z", "y", "x", "c")
    fine = Mesh(mesh.devices.reshape(8, 4, 4, 2), axes)
    placed = (P(axes, None), P(axes, None, None), P(axes, None))
    return jax.shard_map(
        on_device,
        mesh=fine,
        in_specs=placed,
        out_specs=(P(("y", "x", "c"), "z", None), P(("y", "x", "c"), "z", None)),
        check_vma=False,
    )
```

time: 562 us -> 380 us (0.68)
  waiting for transfers between devices: 467 us -> 253 us
  Pallas kernels: 0 us -> 26.8 us
  blocking collectives: 0 us -> 25 us
  matrix products: 25.3 us -> 3.94 us
  local copies, waits for them, and re-layouts: 19.7 us -> 8.53 us
    all_to_all x2 -> x1, waiting for transfers between devices: 285 us -> 7.96 us  [spread(): mine = lax.all_to_all(send, 'y', split_axis=0, concat_axis=0, tiled=True)]
    ppermute x0 -> x22, waiting for transfers between devices: none -> 245 us  [the longest x6 131 us: spread(): lax.ppermute(mine, 'x', shift(chips, step))]
    reduce_scatter x1, waiting for transfers between devices: 182 us -> 0.01 us  [on_device(): act_block = lax.psum_scatter(act_part, 'z', scatter_dimension=0, tiled=True)]
    pallas_call x0 -> x2, Pallas kernels: none -> 26.8 us  [gram(): pl.pallas_call(gram_kernel, out_shape=jax.ShapeDtypeStruct((piece, width)...]
    all_to_all x0 -> x1, blocking collectives: none -> 25 us  [spread(): mine = lax.all_to_all(send, 'y', split_axis=0, concat_axis=0, tiled=True)]
    ppermute x0 -> x22, starting transfers between devices: none -> 23.6 us  [the longest x3 9.76 us: ring_sum(): from_high = lax.ppermute(own_down, 'z', down)]
    dot_general x2 -> x0, matrix products: 23 us -> none  [gram_rows(): lax.dot_general(columns, data, (((0,), (0,)), ((), ())), preferred_elemen...]
    all_to_all x2 -> x1, starting transfers between devices: 23.3 us -> 3.56 us  [spread(): mine = lax.all_to_all(send, 'y', split_axis=0, concat_axis=0, tiled=True)]
  transfers between devices with their start and end apart: 3 -> 24, of which waited for: 3 -> 14; matrix products, arithmetic and copies ran while one was open for 3% -> 6% of each run, Pallas kernels for 0% -> 7%
where the time goes in v1:
time: 380 us; the launch traced here: 373 us
  waiting for transfers between devices  253 us (67%)
  starting transfers between devices  27.2 us (7%)
  Pallas kernels  26.8 us (7%)
  blocking collectives  25 us (7%)
  other arithmetic  14.4 us (4%)
  between operations  14.2 us (4%)
  local copies, waits for them, and re-layouts  8.53 us (2%)
  matrix products  3.94 us (1%)
    ppermute x6, waiting for transfers between devices, spread(): lax.ppermute(mine, 'x', shift(chips, step))  131 us
    ppermute x3, waiting for transfers between devices, ring_sum(): from_low = lax.ppermute(own_up, 'z', up)  42.2 us
    ppermute x3, waiting for transfers between devices, ring_sum(): from_high = lax.ppermute(own_down, 'z', down)  40.8 us
    pallas_call x2, Pallas kernels, gram(): pl.pallas_call(gram_kernel, out_shape=jax.ShapeDtypeStruct((piece, width)...  26.8 us
    all_to_all x1, blocking collectives, spread(): mine = lax.all_to_all(send, 'y', split_axis=0, concat_axis=0, tiled=True)  25 us
    ppermute x1, waiting for transfers between devices, ring_sum(): from_low = lax.ppermute(chunk(far, 0, half), 'z', up)  16.1 us
    ppermute x1, waiting for transfers between devices, ring_sum(): from_high = lax.ppermute(chunk(-far, half, half), 'z', down)  11.6 us
    ppermute x3, starting transfers between devices, ring_sum(): from_high = lax.ppermute(own_down, 'z', down)  9.76 us
  transfers between devices with their start and end apart: 24, of which 14 were waited for; matrix products, arithmetic and copies ran while one was open for 6% of the time, Pallas kernels for 7%

profile of v1, /device:TPU:4, one launch (start us, length us, event | category | flops | bytes accessed | tf_op | source)
XLA Modules:
  0.0 373.2 jit_solution(10708586924180310797)
XLA Ops:
  12.9 25.0 %all_to_all.10 = bf16[4,48,4096]{2,1,0:T(8,128)(2,1)S(1)} all-to-all(bf16[4,48,4096]{2,1,0:T(8,128)(2,1)S(1)} %bitcast.35), channel_id=1, replica_groups=mesh['z'=8,'y'=4,'x'=4,'c'=2] {'y'}, dimensions={0} | all-to-all | bytes 3145728 | tf_op jit(solution)/shard_map/all_to_all | solution.py:92
  39.9 1.7 collective-permute-start.2
  41.6 33.7 %collective-permute-done.refs_1_.refs_9_ = bf16[192,4096]{1,0:T(8,128)(2,1)} collective-permute-done((bf16[192,4096]{1,0:T(8,128)(2,1)S(1)}, bf16[192,4096]{1,0:T(8,128)(2,1)}, u32[]{:S(2)}, u32[]{:S(2)}) %collective-permute-start) | collective-permute-done | bytes 1572896 | tf_op jit(solution)/shard_map/ppermute | solution.py:95
  76.5 30.1 %collective-permute-done.2.refs_3_.refs_11_ = bf16[192,4096]{1,0:T(8,128)(2,1)} collective-permute-done((bf16[192,4096]{1,0:T(8,128)(2,1)S(1)}, bf16[192,4096]{1,0:T(8,128)(2,1)}, u32[]{:S(2)}, u32[]{:S(2)}) %collective-permute-start.2) | collective-permute-done | bytes 1572896 | tf_op jit(solution)/shard_map/ppermute | solution.py:95
  106.6 4.1 %reshape.113 = bf16[256,4096]{1,0:T(8,128)(2,1)} reshape(bf16[128,2,4096]{2,1,0:T(2,128)(2,1)} %param.4) | data formatting | bytes 4194304 | tf_op jit(solution)/shard_map/reshape | solution.py:119
  110.8 3.3 convolution_convert_fusion
  114.1 3.6 all-to-all-start.1
  117.8 13.5 %shard_map.50 = f32[512,4096]{1,0:T(8,128)} custom-call(s32[1]{0:T(128)} %bitcast.strip_ref, bf16[192,4096]{1,0:T(8,128)(2,1)S(1)} %bitcast.32, bf16[192,4096]{1,0:T(8,128)(2,1)} %collective-permute-done.refs_1_.refs_9_, bf16[192,4096]{1,0:T(8,128)(2,1)} %collective-permute-done.1.refs_2_.refs_10_, ...), custom_call_target="tpu_custom_call" | custom-call | flops 6442450944 | bytes 20971520 | tf_op jit(solution)/shard_map/pallas_call | solution.py:44
  131.4 8.0 %all-to-all-done.1 = bf16[4,48,4096]{2,1,0:T(8,128)(2,1)S(1)} async-done(((bf16[4,48,4096]{2,1,0:T(8,128)(2,1)}), bf16[4,48,4096]{2,1,0:T(8,128)(2,1)S(1)}, u32[]{:S(2)}, u32[]{:S(2)}) %all-to-all-start.1) | async-done | bytes 1572896 | tf_op jit(solution)/shard_map/all_to_all | solution.py:92
  139.3 2.6 collective-permute-start.7
  142.0 3.3 collective-permute-start.9
  145.3 31.5 %collective-permute-done.7.refs_1_.refs_9_ = bf16[192,4096]{1,0:T(8,128)(2,1)S(1)} collective-permute-done((bf16[192,4096]{1,0:T(8,128)(2,1)S(1)}, bf16[192,4096]{1,0:T(8,128)(2,1)S(1)}, u32[]{:S(2)}, u32[]{:S(2)}) %collective-permute-start.7) | collective-permute-done | bytes 1572896 | tf_op jit(solution)/shard_map/ppermute | solution.py:95
  176.8 2.6 collective-permute-done.8.refs_2_.refs_10_
  179.4 31.6 %collective-permute-done.9.refs_3_.refs_11_ = bf16[192,4096]{1,0:T(8,128)(2,1)} collective-permute-done((bf16[192,4096]{1,0:T(8,128)(2,1)S(1)}, bf16[192,4096]{1,0:T(8,128)(2,1)}, u32[]{:S(2)}, u32[]{:S(2)}) %collective-permute-start.9) | collective-permute-done | bytes 1572896 | tf_op jit(solution)/shard_map/ppermute | solution.py:95
  211.0 3.7 collective-permute-done.13.refs_7_.refs_15_
  214.8 13.3 %shard_map.51 = f32[512,4096]{1,0:T(8,128)} custom-call(s32[1]{0:T(128)} %bitcast.strip_ref, bf16[192,4096]{1,0:T(8,128)(2,1)S(1)} %bitcast.26, bf16[192,4096]{1,0:T(8,128)(2,1)S(1)} %collective-permute-done.7.refs_1_.refs_9_, bf16[192,4096]{1,0:T(8,128)(2,1)} %collective-permute-done.8.refs_2_.refs_10_, ...), custom_call_target="tpu_custom_call" | custom-call | flops 6442450944 | bytes 20971520 | tf_op jit(solution)/shard_map/pallas_call | solution.py:44
  229.1 2.0 collective-permute-start.14
  231.1 16.1 %collective-permute-done.14 = f32[32,4096]{1,0:T(8,128)S(1)} collective-permute-done((f32[32,4096]{1,0:T(8,128)S(1)}, f32[32,4096]{1,0:T(8,128)S(1)}, u32[]{:S(2)}, u32[]{:S(2)}) %collective-permute-start.14) | collective-permute-done | bytes 524320 | tf_op jit(solution)/shard_map/ppermute | solution.py:76
  247.2 1.7 constant_dynamic-slice_fusion
  248.9 1.8 collective-permute-start.18
  250.7 11.6 %collective-permute-done.18 = f32[32,4096]{1,0:T(8,128)S(1)} collective-permute-done((f32[32,4096]{1,0:T(8,128)S(1)}, f32[32,4096]{1,0:T(8,128)S(1)}, u32[]{:S(2)}, u32[]{:S(2)}) %collective-permute-start.18) | collective-permute-done | bytes 524320 | tf_op jit(solution)/shard_map/ppermute | solution.py:77
  263.5 2.7 collective-permute-start.19
  266.3 20.9 %collective-permute-done.19 = f32[64,4096]{1,0:T(8,128)} collective-permute-done((f32[64,4096]{1,0:T(8,128)S(1)}, f32[64,4096]{1,0:T(8,128)}, u32[]{:S(2)}, u32[]{:S(2)}) %collective-permute-start.19) | collective-permute-done | bytes 1048608 | tf_op jit(solution)/shard_map/ppermute | solution.py:86
  287.3 1.6 dynamic-slice_add_fusion
  288.9 3.6 collective-permute-start.20
  292.5 19.9 %collective-permute-done.20 = f32[64,4096]{1,0:T(8,128)S(1)} collective-permute-done((f32[64,4096]{1,0:T(8,128)S(1)}, f32[64,4096]{1,0:T(8,128)S(1)}, u32[]{:S(2)}, u32[]{:S(2)}) %collective-permute-start.20) | collective-permute-done | bytes 1048608 | tf_op jit(solution)/shard_map/ppermute | solution.py:86
  312.4 3.4 dynamic-slice_add_fusion.1
  316.1 3.5 collective-permute-start.21
  319.5 19.9 %collective-permute-done.16 = f32[64,4096]{1,0:T(8,128)S(1)} collective-permute-done((f32[64,4096]{1,0:T(8,128)}, f32[64,4096]{1,0:T(8,128)S(1)}, u32[]{:S(2)}, u32[]{:S(2)}) %collective-permute-start.16) | collective-permute-done | bytes 1048608 | tf_op jit(solution)/shard_map/ppermute | solution.py:85
  339.5 2.3 dynamic-slice_add_fusion.3
  341.8 22.2 %collective-permute-done.17 = f32[64,4096]{1,0:T(8,128)S(1)} collective-permute-done((f32[64,4096]{1,0:T(8,128)}, f32[64,4096]{1,0:T(8,128)S(1)}, u32[]{:S(2)}, u32[]{:S(2)}) %collective-permute-start.17) | collective-permute-done | bytes 1048608 | tf_op jit(solution)/shard_map/ppermute | solution.py:85
  364.0 2.3 add_bitcast_fusion
  (59 shorter events, 11.7 us)
Async XLA Ops:
  7.2 5.1 %copy-start = (bf16[128,4096]{1,0:T(8,128)(2,1)S(1)}, bf16[128,4096]{1,0:T(8,128)(2,1)}, u32[]{:S(2)}) copy-start(bf16[128,4096]{1,0:T(8,128)(2,1)} %param.3) | copy-start | bytes 3145732
  37.9 37.4 %collective-permute-start = (bf16[192,4096]{1,0:T(8,128)(2,1)S(1)}, bf16[192,4096]{1,0:T(8,128)(2,1)}, u32[]{:S(2)}, u32[]{:S(2)}) collective-permute-start(bf16[192,4096]{1,0:T(8,128)(2,1)S(1)} %bitcast.28), channel_id=1, source_target_pairs={{0,2},{2,4},{4,6},{6,0},{1,3},{3,5},{5,7},{7,1},{8,10},{10,12},{12... | collective-permute-start | bytes 4718600 | tf_op jit(solution)/shard_map/ppermute | solution.py:95
  39.1 37.4 %collective-permute-start.1 = (bf16[192,4096]{1,0:T(8,128)(2,1)S(1)}, bf16[192,4096]{1,0:T(8,128)(2,1)}, u32[]{:S(2)}, u32[]{:S(2)}) collective-permute-start(bf16[192,4096]{1,0:T(8,128)(2,1)S(1)} %bitcast.29), channel_id=1, source_target_pairs={{0,6},{2,0},{4,2},{6,4},{1,7},{3,1},{5,3},{7,5},{8,14},{10,8},{12,... | collective-permute-start | bytes 4718600 | tf_op jit(solution)/shard_map/ppermute | solution.py:95
  39.9 66.7 %collective-permute-start.2 = (bf16[192,4096]{1,0:T(8,128)(2,1)S(1)}, bf16[192,4096]{1,0:T(8,128)(2,1)}, u32[]{:S(2)}, u32[]{:S(2)}) collective-permute-start(bf16[192,4096]{1,0:T(8,128)(2,1)S(1)} %bitcast.30), channel_id=1, source_target_pairs={{0,4},{2,6},{4,0},{6,2},{1,5},{3,7},{5,1},{7,3},{8,12},{10,14},{12... | collective-permute-start | bytes 4718600 | tf_op jit(solution)/shard_map/ppermute | solution.py:95
  41.6 76.1 %collective-permute-start.3 = (bf16[192,4096]{1,0:T(8,128)(2,1)S(1)}, bf16[192,4096]{1,0:T(8,128)(2,1)}, u32[]{:S(2)}, u32[]{:S(2)}) collective-permute-start(bf16[192,4096]{1,0:T(8,128)(2,1)S(1)} %bitcast.31), channel_id=1, source_target_pairs={{0,1},{1,0},{2,3},{3,2},{4,5},{5,4},{6,7},{7,6},{8,9},{9,8},{10,11... | collective-permute-start | bytes 4718600 | tf_op jit(solution)/shard_map/ppermute | solution.py:96
  75.3 42.5 %collective-permute-start.4 = (bf16[192,4096]{1,0:T(8,128)(2,1)}, bf16[192,4096]{1,0:T(8,128)(2,1)}, u32[]{:S(2)}, u32[]{:S(2)}) collective-permute-start(bf16[192,4096]{1,0:T(8,128)(2,1)} %collective-permute-done.refs_1_.refs_9_), channel_id=1, source_target_pairs={{0,1},{1,0},{2,3},{3,2},{4,5},{5,4},{6,7},{7,6},{8,9},{9,8},{10,11... | collective-permute-start | bytes 4718600 | tf_op jit(solution)/shard_map/ppermute | solution.py:96
  76.5 41.3 %collective-permute-start.5 = (bf16[192,4096]{1,0:T(8,128)(2,1)}, bf16[192,4096]{1,0:T(8,128)(2,1)}, u32[]{:S(2)}, u32[]{:S(2)}) collective-permute-start(bf16[192,4096]{1,0:T(8,128)(2,1)} %collective-permute-done.1.refs_2_.refs_10_), channel_id=1, source_target_pairs={{0,1},{1,0},{2,3},{3,2},{4,5},{5,4},{6,7},{7,6},{8,9},{9,8},{10,11... | collective-permute-start | bytes 4718600 | tf_op jit(solution)/shard_map/ppermute | solution.py:96
  106.6 11.2 %collective-permute-start.6 = (bf16[192,4096]{1,0:T(8,128)(2,1)}, bf16[192,4096]{1,0:T(8,128)(2,1)}, u32[]{:S(2)}, u32[]{:S(2)}) collective-permute-start(bf16[192,4096]{1,0:T(8,128)(2,1)} %collective-permute-done.2.refs_3_.refs_11_), channel_id=1, source_target_pairs={{0,1},{1,0},{2,3},{3,2},{4,5},{5,4},{6,7},{7,6},{8,9},{9,8},{10,11... | collective-permute-start | bytes 4718600 | tf_op jit(solution)/shard_map/ppermute | solution.py:96
  114.1 25.2 %all-to-all-start.1 = ((bf16[4,48,4096]{2,1,0:T(8,128)(2,1)}), bf16[4,48,4096]{2,1,0:T(8,128)(2,1)S(1)}, u32[]{:S(2)}, u32[]{:S(2)}) async-start(bf16[4,48,4096]{2,1,0:T(8,128)(2,1)} %bitcast.34), calls=%async_computation.2 | async-start | bytes 3145728 | tf_op jit(solution)/shard_map/all_to_all | solution.py:92
  117.7 248.6 %reduce-scatter.2.cloned.1.call-start = ((), (), s32[]{:S(2)}) async-start(), calls=%async_computation.3 | async-start | bytes 9437184 | tf_op jit(solution)/shard_map/reduce_scatter | solution.py:124
  139.3 37.5 %collective-permute-start.7 = (bf16[192,4096]{1,0:T(8,128)(2,1)S(1)}, bf16[192,4096]{1,0:T(8,128)(2,1)S(1)}, u32[]{:S(2)}, u32[]{:S(2)}) collective-permute-start(bf16[192,4096]{1,0:T(8,128)(2,1)S(1)} %bitcast.22), channel_id=1, source_target_pairs={{0,2},{2,4},{4,6},{6,0},{1,3},{3,5},{5,7},{7,1},{8,10},{10,12},{12... | collective-permute-start | bytes 4718600 | tf_op jit(solution)/shard_map/ppermute | solution.py:95
  142.0 37.4 %collective-permute-start.8 = (bf16[192,4096]{1,0:T(8,128)(2,1)S(1)}, bf16[192,4096]{1,0:T(8,128)(2,1)}, u32[]{:S(2)}, u32[]{:S(2)}) collective-permute-start(bf16[192,4096]{1,0:T(8,128)(2,1)S(1)} %bitcast.23), channel_id=1, source_target_pairs={{0,6},{2,0},{4,2},{6,4},{1,7},{3,1},{5,3},{7,5},{8,14},{10,8},{12,... | collective-permute-start | bytes 4718600 | tf_op jit(solution)/shard_map/ppermute | solution.py:95
  142.0 69.0 %collective-permute-start.9 = (bf16[192,4096]{1,0:T(8,128)(2,1)S(1)}, bf16[192,4096]{1,0:T(8,128)(2,1)}, u32[]{:S(2)}, u32[]{:S(2)}) collective-permute-start(bf16[192,4096]{1,0:T(8,128)(2,1)S(1)} %bitcast.24), channel_id=1, source_target_pairs={{0,4},{2,6},{4,0},{6,2},{1,5},{3,7},{5,1},{7,3},{8,12},{10,14},{12... | collective-permute-start | bytes 4718600 | tf_op jit(solution)/shard_map/ppermute | solution.py:95
  145.3 65.7 %collective-permute-start.10 = (bf16[192,4096]{1,0:T(8,128)(2,1)S(1)}, bf16[192,4096]{1,0:T(8,128)(2,1)}, u32[]{:S(2)}, u32[]{:S(2)}) collective-permute-start(bf16[192,4096]{1,0:T(8,128)(2,1)S(1)} %bitcast.25), channel_id=1, source_target_pairs={{0,1},{1,0},{2,3},{3,2},{4,5},{5,4},{6,7},{7,6},{8,9},{9,8},{10,11... | collective-permute-start | bytes 4718600 | tf_op jit(solution)/shard_map/ppermute | solution.py:96
  176.8 34.2 %collective-permute-start.11 = (bf16[192,4096]{1,0:T(8,128)(2,1)S(1)}, bf16[192,4096]{1,0:T(8,128)(2,1)}, u32[]{:S(2)}, u32[]{:S(2)}) collective-permute-start(bf16[192,4096]{1,0:T(8,128)(2,1)S(1)} %collective-permute-done.7.refs_1_.refs_9_), channel_id=1, source_target_pairs={{0,1},{1,0},{2,3},{3,2},{4,5},{5,4},{6,7},{7,6},{8,9},{9,8},{10,11... | collective-permute-start | bytes 4718600 | tf_op jit(solution)/shard_map/ppermute | solution.py:96
  179.4 31.6 %collective-permute-start.12 = (bf16[192,4096]{1,0:T(8,128)(2,1)}, bf16[192,4096]{1,0:T(8,128)(2,1)}, u32[]{:S(2)}, u32[]{:S(2)}) collective-permute-start(bf16[192,4096]{1,0:T(8,128)(2,1)} %collective-permute-done.8.refs_2_.refs_10_), channel_id=1, source_target_pairs={{0,1},{1,0},{2,3},{3,2},{4,5},{5,4},{6,7},{7,6},{8,9},{9,8},{10,11... | collective-permute-start | bytes 4718600 | tf_op jit(solution)/shard_map/ppermute | solution.py:96
  211.0 3.8 %collective-permute-start.13 = (bf16[192,4096]{1,0:T(8,128)(2,1)}, bf16[192,4096]{1,0:T(8,128)(2,1)}, u32[]{:S(2)}, u32[]{:S(2)}) collective-permute-start(bf16[192,4096]{1,0:T(8,128)(2,1)} %collective-permute-done.9.refs_3_.refs_11_), channel_id=1, source_target_pairs={{0,1},{1,0},{2,3},{3,2},{4,5},{5,4},{6,7},{7,6},{8,9},{9,8},{10,11... | collective-permute-start | bytes 4718600 | tf_op jit(solution)/shard_map/ppermute | solution.py:96
  229.1 18.1 %collective-permute-start.14 = (f32[32,4096]{1,0:T(8,128)S(1)}, f32[32,4096]{1,0:T(8,128)S(1)}, u32[]{:S(2)}, u32[]{:S(2)}) collective-permute-start(f32[32,4096]{1,0:T(8,128)S(1)} %constant_dynamic-slice_fusion.2), channel_id=1, source_target_pairs={{0,32},{32,64},{64,96},{96,128},{128,160},{160,192},{192,224},{224... | collective-permute-start | bytes 1572872 | tf_op jit(solution)/shard_map/ppermute | solution.py:76
  248.9 13.4 %collective-permute-start.18 = (f32[32,4096]{1,0:T(8,128)S(1)}, f32[32,4096]{1,0:T(8,128)S(1)}, u32[]{:S(2)}, u32[]{:S(2)}) collective-permute-start(f32[32,4096]{1,0:T(8,128)S(1)} %get-tuple-element.6), channel_id=1, source_target_pairs={{0,224},{32,0},{64,32},{96,64},{128,96},{160,128},{192,160},{224,1... | collective-permute-start | bytes 1572872 | tf_op jit(solution)/shard_map/ppermute | solution.py:77
  263.5 23.8 %collective-permute-start.19 = (f32[64,4096]{1,0:T(8,128)S(1)}, f32[64,4096]{1,0:T(8,128)}, u32[]{:S(2)}, u32[]{:S(2)}) collective-permute-start(f32[64,4096]{1,0:T(8,128)S(1)} %pad_maximum_fusion.1), channel_id=1, source_target_pairs={{0,224},{32,0},{64,32},{96,64},{128,96},{160,128},{192,160},{224,1... | collective-permute-start | bytes 3145736 | tf_op jit(solution)/shard_map/ppermute | solution.py:86
  266.2 26.3 %collective-permute-start.15 = (f32[64,4096]{1,0:T(8,128)S(1)}, f32[64,4096]{1,0:T(8,128)}, u32[]{:S(2)}, u32[]{:S(2)}) collective-permute-start(f32[64,4096]{1,0:T(8,128)S(1)} %pad_maximum_fusion), channel_id=1, source_target_pairs={{0,32},{32,64},{64,96},{96,128},{128,160},{160,192},{192,224},{224... | collective-permute-start | bytes 3145736 | tf_op jit(solution)/shard_map/ppermute | solution.py:85
  288.9 23.5 %collective-permute-start.20 = (f32[64,4096]{1,0:T(8,128)S(1)}, f32[64,4096]{1,0:T(8,128)S(1)}, u32[]{:S(2)}, u32[]{:S(2)}) collective-permute-start(f32[64,4096]{1,0:T(8,128)S(1)} %dynamic-slice_add_fusion), channel_id=1, source_target_pairs={{0,224},{32,0},{64,32},{96,64},{128,96},{160,128},{192,160},{224,1... | collective-permute-start | bytes 3145736 | tf_op jit(solution)/shard_map/ppermute | solution.py:86
  315.8 23.6 %collective-permute-start.16 = (f32[64,4096]{1,0:T(8,128)}, f32[64,4096]{1,0:T(8,128)S(1)}, u32[]{:S(2)}, u32[]{:S(2)}) collective-permute-start(f32[64,4096]{1,0:T(8,128)} %get-tuple-element.3), channel_id=1, source_target_pairs={{0,32},{32,64},{64,96},{96,128},{128,160},{160,192},{192,224},{224... | collective-permute-start | bytes 3145736 | tf_op jit(solution)/shard_map/ppermute | solution.py:85
  316.1 25.7 %collective-permute-start.21 = (f32[64,4096]{1,0:T(8,128)}, f32[64,4096]{1,0:T(8,128)S(1)}, u32[]{:S(2)}, u32[]{:S(2)}) collective-permute-start(f32[64,4096]{1,0:T(8,128)} %get-tuple-element.2), channel_id=1, source_target_pairs={{0,224},{32,0},{64,32},{96,64},{128,96},{160,128},{192,160},{224,1... | collective-permute-start | bytes 3145736 | tf_op jit(solution)/shard_map/ppermute | solution.py:86
  341.8 22.2 %collective-permute-start.17 = (f32[64,4096]{1,0:T(8,128)}, f32[64,4096]{1,0:T(8,128)S(1)}, u32[]{:S(2)}, u32[]{:S(2)}) collective-permute-start(f32[64,4096]{1,0:T(8,128)} %dynamic-slice_add_fusion.3), channel_id=1, source_target_pairs={{0,32},{32,64},{64,96},{96,128},{128,160},{160,192},{192,224},{224... | collective-permute-start | bytes 3145736 | tf_op jit(solution)/shard_map/ppermute | solution.py:85
  341.8 24.6 %copy-start.1 = (bf16[128,4096]{1,0:T(8,128)(2,1)S(1)}, bf16[128,4096]{1,0:T(8,128)(2,1)}, u32[]{:S(2)}) copy-start(bf16[128,4096]{1,0:T(8,128)(2,1)} %param.3) | copy-start | bytes 3145732
Sparse Core Ops, SparseCore 0:
  131.5 99.7 reduce-scatter.1

commit v2 on v1

v2 whole, which is shorter than its diff:
```python
import jax
import jax.numpy as jnp
from jax import lax
from jax.experimental import pallas as pl
from jax.experimental.pallas import tpu as pltpu
from jax.sharding import Mesh, PartitionSpec as P

EXPERTS = 8
TOP = 2
EXP_WIN = 4
CAP = 48
TILE = 512
LANES = 128
ROWS = 16
FINE = 128.0
LEVELS = 32767.0


def shift(size, step):
    return [(i, (i + step) % size) for i in range(size)]


def gram_kernel(strip_ref, *refs):
    blocks = (len(refs) - 3) // 2
    left_refs, right_refs = refs[:blocks], refs[blocks : 2 * blocks]
    out_ref, left, right = refs[2 * blocks :]

    def stack(into, parts):
        at = 0
        for part in parts:
            into[at : at + part.shape[0], :] = part[...]
            at += part.shape[0]

    @pl.when(pl.program_id(0) == 0)
    def _():
        stack(left, left_refs)

    stack(right, right_refs)
    out_ref[...] = lax.dot_general(
        left[...], right[...], (((0,), (0,)), ((), ())), preferred_element_type=jnp.float32
    )


def gram(strip, blocks, piece):
    width = blocks[0].shape[1]
    rows = sum(block.shape[0] for block in blocks)
    return pl.pallas_call(
        gram_kernel,
        out_shape=jax.ShapeDtypeStruct((piece, width), jnp.float32),
        grid_spec=pltpu.PrefetchScalarGridSpec(
            num_scalar_prefetch=1,
            grid=(width // TILE,),
            in_specs=[pl.BlockSpec((b.shape[0], piece), lambda j, s: (0, s[0])) for b in blocks]
            + [pl.BlockSpec((b.shape[0], TILE), lambda j, s: (0, j)) for b in blocks],
            out_specs=pl.BlockSpec((piece, TILE), lambda j, s: (0, j)),
            scratch_shapes=[
                pltpu.VMEM((rows, piece), jnp.bfloat16),
                pltpu.VMEM((rows, TILE), jnp.bfloat16),
            ],
        ),
        compiler_params=pltpu.CompilerParams(vmem_limit_bytes=40 * 2**20),
        cost_estimate=pl.CostEstimate(
            flops=2 * rows * piece * width,
            bytes_accessed=rows * width * 2 + piece * width * 4,
            transcendentals=0,
        ),
    )(strip, *blocks, *blocks)


def encode(values, out_ref):
    rows, width = values.shape
    lane = lax.broadcasted_iota(jnp.int32, (rows, LANES), 1)
    top = jnp.zeros((rows, LANES), jnp.float32)
    for b in range(width // LANES):
        most = jnp.max(jnp.abs(values[:, b * LANES : (b + 1) * LANES]), axis=1, keepdims=True)
        top = jnp.where(lane == b, most, top)
    code = jnp.ceil(jnp.log2(jnp.maximum(top, 2.0**-126)) * FINE)
    shrink = jnp.exp2(code * (-1.0 / FINE))
    out_ref[:, width:] = code.astype(jnp.int32).astype(jnp.int16)
    for b in range(width // LANES):
        cut = slice(b * LANES, (b + 1) * LANES)
        level = jnp.round(values[:, cut] * shrink[:, b : b + 1] * LEVELS)
        level = jnp.clip(level, -LEVELS, LEVELS)
        out_ref[:, cut] = level.astype(jnp.int32).astype(jnp.int16)


def add_decoded(total, coded_ref):
    rows, width = total.shape
    code = coded_ref[:, width:].astype(jnp.int32).astype(jnp.float32)
    unit = jnp.exp2(code * (1.0 / FINE)) * (1.0 / LEVELS)
    for b in range(width // LANES):
        cut = slice(b * LANES, (b + 1) * LANES)
        total[:, cut] += coded_ref[:, cut].astype(jnp.int32).astype(jnp.float32) * unit[:, b : b + 1]


def first_kernel(at_ref, up_own, down_own, up_out, down_out):
    encode(up_own, up_out)
    encode(down_own, down_out)


def step_kernel(at_ref, up_own, down_own, up_in, down_in, up_out, down_out, total):
    halved = at_ref[2] == 1
    i = pl.program_id(0)
    half = pl.num_programs(0) // 2
    for own, got, out, here in (
        (up_own, up_in, up_out, jnp.logical_or(jnp.logical_not(halved), i < half)),
        (down_own, down_in, down_out, jnp.logical_or(jnp.logical_not(halved), i >= half)),
    ):
        total[...] = own[...]

        @pl.when(here)
        def _():
            add_decoded(total, got)

        encode(total, out)


def last_kernel(at_ref, scale_ref, own, up_in, down_in, out_ref):
    out_ref[...] = own[...]
    add_decoded(out_ref, up_in)
    add_decoded(out_ref, down_in)
    out_ref[...] = out_ref[...] * scale_ref[0]


def ring_sum(part, groups, scale):
    z = lax.axis_index("z").astype(jnp.int32)
    width = part.shape[1]
    rows = part.shape[0] // groups
    bands = rows // ROWS
    far = groups // 2
    up, down = shift(groups, 1), shift(groups, -1)

    def place(step):
        return lax.rem(z + step + groups, groups) * bands

    def own(k):
        return pl.BlockSpec((ROWS, width), lambda i, at: (at[k] + i, 0))

    def coded(fn):
        return pl.BlockSpec((ROWS, width + LANES), lambda i, at: (fn(i), 0))

    def call(kernel, at, bands, ins, in_specs, scratch=()):
        return pl.pallas_call(
            kernel,
            out_shape=[jax.ShapeDtypeStruct((bands * ROWS, width + LANES), jnp.int16)] * 2,
            grid_spec=pltpu.PrefetchScalarGridSpec(
                num_scalar_prefetch=1,
                grid=(bands,),
                in_specs=in_specs,
                out_specs=[coded(lambda i: i)] * 2,
                scratch_shapes=list(scratch),
            ),
            cost_estimate=pl.CostEstimate(
                flops=16 * bands * ROWS * width,
                bytes_accessed=16 * bands * ROWS * width,
                transcendentals=0,
            ),
        )(at, *ins)

    sends = call(
        first_kernel,
        jnp.stack([place(far), place(far) + bands // 2]),
        bands // 2,
        (part, part),
        [own(0), own(1)],
    )
    for step in range(far - 1, 0, -1):
        got = lax.ppermute(sends[0], "z", up), lax.ppermute(sends[1], "z", down)
        halved = step == far - 1
        half = bands // 2
        specs = (
            [coded(lambda i: jnp.minimum(i, half - 1)), coded(lambda i: jnp.maximum(i - half, 0))]
            if halved
            else [coded(lambda i: i)] * 2
        )
        sends = call(
            step_kernel,
            jnp.stack([place(step), place(-step), jnp.int32(halved)]),
            bands,
            (part, part) + got,
            [own(0), own(1)] + specs,
            [pltpu.VMEM((ROWS, width), jnp.float32)],
        )
    got = lax.ppermute(sends[0], "z", up), lax.ppermute(sends[1], "z", down)
    return pl.pallas_call(
        last_kernel,
        out_shape=jax.ShapeDtypeStruct((rows, width), jnp.float32),
        grid_spec=pltpu.PrefetchScalarGridSpec(
            num_scalar_prefetch=2,
            grid=(bands,),
            in_specs=[
                pl.BlockSpec((ROWS, width), lambda i, at, s: (at[0] + i, 0)),
                pl.BlockSpec((ROWS, width + LANES), lambda i, at, s: (i, 0)),
                pl.BlockSpec((ROWS, width + LANES), lambda i, at, s: (i, 0)),
            ],
            out_specs=pl.BlockSpec((ROWS, width), lambda i, at, s: (i, 0)),
        ),
        cost_estimate=pl.CostEstimate(
            flops=16 * rows * width, bytes_accessed=12 * rows * width, transcendentals=0
        ),
    )(place(0).reshape(1), jnp.full((1,), scale, jnp.float32), part, *got)


def exchange(sends, axis):
    chips = lax.axis_size(axis)
    order = (1, chips - 1, 2)
    return [sends[0]] + [lax.ppermute(sends[d], axis, shift(chips, d)) for d in order]


def gather(blocks, axis):
    chips = lax.axis_size(axis)
    up, down = shift(chips, 1), shift(chips, -1)
    half = len(blocks) // 2
    low = jnp.concatenate(blocks[:half], axis=0)
    high = jnp.concatenate(blocks[half:], axis=0)
    low_up = lax.ppermute(low, axis, up)
    high_down = lax.ppermute(high, axis, down)
    high_up = lax.ppermute(high, axis, up)
    low_down = lax.ppermute(low, axis, down)
    low_far = lax.ppermute(low_up, axis, up)
    high_far = lax.ppermute(high_down, axis, down)
    held = [low, high, low_up, high_down, high_up, low_down, low_far, high_far]
    return held + [lax.ppermute(block, "c", shift(2, 1)) for block in held]


def on_device(activations, out_grads, routes):
    tok_rows = activations.shape[0]
    width = activations.shape[1]
    groups = lax.axis_size("z")
    chips = lax.axis_size("x")
    split = chips * lax.axis_size("c")
    piece = width // split
    scale_norm = tok_rows * groups * EXP_WIN * split * TOP / EXPERTS
    x, y, core = (lax.axis_index(axis).astype(jnp.int32) for axis in ("x", "y", "c"))
    flat_grads = out_grads.reshape(TOP * tok_rows, width)
    flat_routes = routes.reshape(TOP * tok_rows)

    def placing(first):
        experts = lax.rem(first + jnp.arange(EXP_WIN, dtype=jnp.int32), EXP_WIN)
        hits = (flat_routes[None, :] == experts[:, None]).astype(jnp.int32)
        slots = jnp.cumsum(hits, axis=1) - hits
        slot = jnp.arange(CAP, dtype=jnp.int32)
        chosen = (slots[:, None, :] == slot[None, :, None]) & (hits[:, None, :] == 1)
        return chosen.reshape(EXP_WIN * CAP, TOP * tok_rows)

    def pack(rows, data):
        sent = jnp.dot(rows.astype(jnp.bfloat16), data, preferred_element_type=jnp.float32)
        return sent.astype(jnp.bfloat16).reshape(EXP_WIN, CAP, width)

    act_rows = placing(y).reshape(EXP_WIN * CAP, tok_rows, TOP).any(axis=-1)
    send_act = pack(act_rows, activations)
    send_grad = pack(placing(x), flat_grads)

    act = jnp.concatenate(exchange(send_act, "y"), axis=0)
    grad = exchange(send_grad, "x")
    act = lax.all_gather(act, ("x", "c"), tiled=True)
    grad = gather(grad, "y")
    grad_strip = lax.rem(x + y, chips) * 2 + core
    grad_part = gram(grad_strip.reshape(1), grad, piece)
    act_part = gram((x * 2 + core).reshape(1), [act], piece)
    grad_block = ring_sum(grad_part, groups, 1.0 / scale_norm)
    act_block = ring_sum(act_part, groups, 1.0 / scale_norm)
    moves = [
        (b * chips + a, a * chips + (a + b) % chips) for b in range(chips) for a in range(chips)
    ]
    grad_block = lax.ppermute(grad_block, ("y", "x"), moves)
    return act_block[None], grad_block[None]


def solution(mesh):
    axes = ("z", "y", "x", "c")
    fine = Mesh(mesh.devices.reshape(8, 4, 4, 2), axes)
    placed = (P(axes, None), P(axes, None, None), P(axes, None))
    return jax.shard_map(
        on_device,
        mesh=fine,
        in_specs=placed,
        out_specs=(P(("y", "x", "c"), "z", None), P(("y", "x", "c"), "z", None)),
        check_vma=False,
    )
```

time: 380 us -> 306 us (0.81)
  waiting for transfers between devices: 253 us -> 109 us
  Pallas kernels: 26.8 us -> 81.3 us
  starting transfers between devices: 27.2 us -> 61.1 us
  blocking collectives: 25 us -> 0 us
  local copies, waits for them, and re-layouts: 8.53 us -> 26.7 us
  other arithmetic: 14.4 us -> 7.33 us
    ppermute x22 -> x37, waiting for transfers between devices: 245 us -> 109 us  [the longest x6 37.5 us: exchange(): lax.ppermute(sends[d], axis, shift(chips, d))]
    pallas_call x0 -> x10, Pallas kernels: none -> 56.4 us  [the longest x8 48.1 us: call(): pl.pallas_call(kernel, out_shape=[jax.ShapeDtypeStruct((bands * ROWS, wid...]
    ppermute x22 -> x37, starting transfers between devices: 23.6 us -> 61.1 us  [the longest x16 40.1 us: ring_sum(): got = (lax.ppermute(sends[0], 'z', up), lax.ppermute(sends[1], 'z', down))]
    all_to_all x1 -> x0, blocking collectives: 25 us -> none  [spread(): mine = lax.all_to_all(send, 'y', split_axis=0, concat_axis=0, tiled=True)]
    unnamed x7 -> x49, local copies, waits for them, and re-layouts: 1.16 us -> 21 us
    add x4 -> x0, other arithmetic: 8.45 us -> none  [the longest x3 7.36 us: ring_sum(): own_up, own_down = (own_up + from_low, own_down + from_high)]
    all_to_all x1 -> x0, waiting for transfers between devices: 7.96 us -> none  [spread(): mine = lax.all_to_all(send, 'y', split_axis=0, concat_axis=0, tiled=True)]
  transfers between devices with their start and end apart: 24 -> 38, of which waited for: 14 -> 16; matrix products, arithmetic and copies ran while one was open for 6% -> 2% of each run, Pallas kernels for 7% -> 26%
where the time goes in v2:
time: 306 us; the launch traced here: 301 us
  waiting for transfers between devices  109 us (36%)
  Pallas kernels  81.3 us (27%)
  starting transfers between devices  61.1 us (20%)
  local copies, waits for them, and re-layouts  26.7 us (9%)
  between operations  14.5 us (5%)
  other arithmetic  7.33 us (2%)
    pallas_call x8, Pallas kernels, call(): pl.pallas_call(kernel, out_shape=[jax.ShapeDtypeStruct((bands * ROWS, wid...  48.1 us
    ppermute x16, starting transfers between devices, ring_sum(): got = (lax.ppermute(sends[0], 'z', up), lax.ppermute(sends[1], 'z', down))  40.1 us
    ppermute x6, waiting for transfers between devices, exchange(): lax.ppermute(sends[d], axis, shift(chips, d))  37.5 us
    pallas_call x2, Pallas kernels, gram(): pl.pallas_call(gram_kernel, out_shape=jax.ShapeDtypeStruct((piece, width)...  24.9 us
    ppermute x16, waiting for transfers between devices, ring_sum(): got = (lax.ppermute(sends[0], 'z', up), lax.ppermute(sends[1], 'z', down))  24.3 us
    unnamed x49, local copies, waits for them, and re-layouts  21 us
    ppermute x1, waiting for transfers between devices, gather(): low_far = lax.ppermute(low_up, axis, up)  14.3 us
    ppermute x1, waiting for transfers between devices, gather(): high_down = lax.ppermute(high, axis, down)  12.9 us
  transfers between devices with their start and end apart: 38, of which 16 were waited for; matrix products, arithmetic and copies ran while one was open for 2% of the time, Pallas kernels for 26%

profile of v2, /device:TPU:4, one launch (start us, length us, event | category | flops | bytes accessed | tf_op | source)
XLA Modules:
  0.0 300.8 jit_solution(6100409588216570120)
XLA Ops:
  14.9 3.3 %collective-permute-start.2 = (bf16[48,4096]{1,0:T(8,128)(2,1)S(1)}, bf16[48,4096]{1,0:T(8,128)(2,1)S(1)}, u32[]{:S(2)}, u32[]{:S(2)}) collective-permute-start(bf16[48,4096]{1,0:T(8,128)(2,1)S(1)} %get-tuple-element.39), channel_id=1, source_target_pairs={{0,16},{8,24},{16,0},{24,8},{1,17},{9,25},{17,1},{25,9},{2,18},{10... | collective-permute-start | bytes 1179656 | tf_op jit(solution)/shard_map/ppermute | solution.py:207
  20.2 8.3 %collective-permute-done.2 = bf16[48,4096]{1,0:T(8,128)(2,1)S(1)} collective-permute-done((bf16[48,4096]{1,0:T(8,128)(2,1)S(1)}, bf16[48,4096]{1,0:T(8,128)(2,1)S(1)}, u32[]{:S(2)}, u32[]{:S(2)}) %collective-permute-start.2) | collective-permute-done | bytes 393248 | tf_op jit(solution)/shard_map/ppermute | solution.py:207
  28.6 7.6 %collective-permute-done.1 = bf16[48,4096]{1,0:T(8,128)(2,1)S(1)} collective-permute-done((bf16[48,4096]{1,0:T(8,128)(2,1)S(1)}, bf16[48,4096]{1,0:T(8,128)(2,1)S(1)}, u32[]{:S(2)}, u32[]{:S(2)}) %collective-permute-start.1) | collective-permute-done | bytes 393248 | tf_op jit(solution)/shard_map/ppermute | solution.py:207
  44.3 8.9 %collective-permute-done.11 = bf16[48,4096]{1,0:T(8,128)(2,1)S(1)} collective-permute-done((bf16[48,4096]{1,0:T(8,128)(2,1)S(1)}, bf16[48,4096]{1,0:T(8,128)(2,1)S(1)}, u32[]{:S(2)}, u32[]{:S(2)}) %collective-permute-start.11) | collective-permute-done | bytes 393248 | tf_op jit(solution)/shard_map/ppermute | solution.py:207
  56.0 12.6 %collective-permute-done.12 = bf16[48,4096]{1,0:T(8,128)(2,1)S(1)} collective-permute-done((bf16[48,4096]{1,0:T(8,128)(2,1)S(1)}, bf16[48,4096]{1,0:T(8,128)(2,1)S(1)}, u32[]{:S(2)}, u32[]{:S(2)}) %collective-permute-start.12) | collective-permute-done | bytes 393248 | tf_op jit(solution)/shard_map/ppermute | solution.py:207
  73.9 3.5 %collective-permute-done.14.refs_2_.refs_18_ = bf16[96,4096]{1,0:T(8,128)(2,1)} collective-permute-done((bf16[96,4096]{1,0:T(8,128)(2,1)S(1)}, bf16[96,4096]{1,0:T(8,128)(2,1)}, u32[]{:S(2)}, u32[]{:S(2)}) %collective-permute-start.14) | collective-permute-done | bytes 786464 | tf_op jit(solution)/shard_map/ppermute | solution.py:216
  77.4 12.9 %collective-permute-done.15.refs_3_.refs_19_ = bf16[96,4096]{1,0:T(8,128)(2,1)} collective-permute-done((bf16[96,4096]{1,0:T(8,128)(2,1)S(1)}, bf16[96,4096]{1,0:T(8,128)(2,1)}, u32[]{:S(2)}, u32[]{:S(2)}) %collective-permute-start.15) | collective-permute-done | bytes 786464 | tf_op jit(solution)/shard_map/ppermute | solution.py:217
  90.3 3.8 %collective-permute-start.19 = (bf16[96,4096]{1,0:T(8,128)(2,1)}, bf16[96,4096]{1,0:T(8,128)(2,1)}, u32[]{:S(2)}, u32[]{:S(2)}) collective-permute-start(bf16[96,4096]{1,0:T(8,128)(2,1)} %collective-permute-done.15.refs_3_.refs_19_), channel_id=1, source_target_pairs={{0,24},{8,0},{16,8},{24,16},{1,25},{9,1},{17,9},{25,17},{2,26},{10... | collective-permute-start | bytes 2359304 | tf_op jit(solution)/shard_map/ppermute | solution.py:221
  96.3 14.3 %collective-permute-done.18.refs_6_.refs_22_ = bf16[96,4096]{1,0:T(8,128)(2,1)} collective-permute-done((bf16[96,4096]{1,0:T(8,128)(2,1)}, bf16[96,4096]{1,0:T(8,128)(2,1)}, u32[]{:S(2)}, u32[]{:S(2)}) %collective-permute-start.18) | collective-permute-done | bytes 786464 | tf_op jit(solution)/shard_map/ppermute | solution.py:220
  116.9 13.1 %shard_map.56.up_own.down_own.own = f32[512,4096]{1,0:T(8,128)} custom-call(s32[1]{0:T(128)} %bitcast.12.strip_ref, bf16[96,4096]{1,0:T(8,128)(2,1)S(1)} %pad_maximum_fusion.1.refs_0_.refs_16_, bf16[96,4096]{1,0:T(8,128)(2,1)S(1)} %constant_dynamic-update-slice_fusion.refs_1_.refs_17_, bf16[96,4096]{1,0:T(8,128)(2,1)} %collective-permute-done.14.refs_2_.refs_18_, ...), custom_call_target="tpu_custom_call" | custom-call | flops 6442450944 | bytes 20971520 | tf_op jit(solution)/shard_map/pallas_call | solution.py:47
  130.0 3.8 %shard_map.57 = (s16[32,4224]{1,0:T(8,128)(2,1)}, s16[32,4224]{1,0:T(8,128)(2,1)}) custom-call(s32[2]{0:T(128)} %pad_add_fusion.3.at_ref, f32[512,4096]{1,0:T(8,128)} %shard_map.56.up_own.down_own.own, f32[512,4096]{1,0:T(8,128)} %shard_map.56.up_own.down_own.own), custom_call_target="tpu_custom_call" | custom-call | flops 2097152 | bytes 2097152 | tf_op jit(solution)/shard_map/pallas_call | solution.py:143
  135.7 6.0 %collective-permute-start.29 = (s16[32,4224]{1,0:T(8,128)(2,1)}, s16[32,4224]{1,0:T(8,128)(2,1)S(1)}, u32[]{:S(2)}, u32[]{:S(2)}) collective-permute-start(s16[32,4224]{1,0:T(8,128)(2,1)} %get-tuple-element.27), channel_id=1, source_target_pairs={{0,224},{32,0},{64,32},{96,64},{128,96},{160,128},{192,160},{224,1... | collective-permute-start | bytes 811016 | tf_op jit(solution)/shard_map/ppermute | solution.py:168
  142.3 6.3 %collective-permute-done.28.up_in = s16[32,4224]{1,0:T(8,128)(2,1)S(1)} collective-permute-done((s16[32,4224]{1,0:T(8,128)(2,1)}, s16[32,4224]{1,0:T(8,128)(2,1)S(1)}, u32[]{:S(2)}, u32[]{:S(2)}) %collective-permute-start.28) | collective-permute-done | bytes 270368 | tf_op jit(solution)/shard_map/ppermute | solution.py:168
  150.0 6.4 %shard_map.58 = (s16[64,4224]{1,0:T(8,128)(2,1)}, s16[64,4224]{1,0:T(8,128)(2,1)}) custom-call(s32[3]{0:T(128)} %pad_add_fusion.2.at_ref, f32[512,4096]{1,0:T(8,128)} %shard_map.56.up_own.down_own.own, f32[512,4096]{1,0:T(8,128)} %shard_map.56.up_own.down_own.own, s16[32,4224]{1,0:T(8,128)(2,1)} %copy-done.19, s16[32,4224]{1,0:T(8,128)(2,1)} %copy-done.20), custom_call_target="tpu_custom_call" | custom-call | flops 4194304 | bytes 4194304 | tf_op jit(solution)/shard_map/pallas_call | solution.py:143
  156.4 3.2 %collective-permute-start.31 = (s16[64,4224]{1,0:T(8,128)(2,1)}, s16[64,4224]{1,0:T(8,128)(2,1)S(1)}, u32[]{:S(2)}, u32[]{:S(2)}) collective-permute-start(s16[64,4224]{1,0:T(8,128)(2,1)} %get-tuple-element.29), channel_id=1, source_target_pairs={{0,224},{32,0},{64,32},{96,64},{128,96},{160,128},{192,160},{224,1... | collective-permute-start | bytes 1622024 | tf_op jit(solution)/shard_map/ppermute | solution.py:168
  160.3 11.4 %collective-permute-done.30.up_in = s16[64,4224]{1,0:T(8,128)(2,1)S(1)} collective-permute-done((s16[64,4224]{1,0:T(8,128)(2,1)}, s16[64,4224]{1,0:T(8,128)(2,1)S(1)}, u32[]{:S(2)}, u32[]{:S(2)}) %collective-permute-start.30) | collective-permute-done | bytes 540704 | tf_op jit(solution)/shard_map/ppermute | solution.py:168
  173.2 6.9 %shard_map.59 = (s16[64,4224]{1,0:T(8,128)(2,1)}, s16[64,4224]{1,0:T(8,128)(2,1)}) custom-call(s32[3]{0:T(128)} %pad_add_fusion.at_ref, f32[512,4096]{1,0:T(8,128)} %shard_map.56.up_own.down_own.own, f32[512,4096]{1,0:T(8,128)} %shard_map.56.up_own.down_own.own, s16[64,4224]{1,0:T(8,128)(2,1)} %copy-done.9, s16[64,4224]{1,0:T(8,128)(2,1)} %copy-done.10), custom_call_target="tpu_custom_call" | custom-call | flops 4194304 | bytes 4194304 | tf_op jit(solution)/shard_map/pallas_call | solution.py:143
  180.2 9.6 %collective-permute-start.32 = (s16[64,4224]{1,0:T(8,128)(2,1)}, s16[64,4224]{1,0:T(8,128)(2,1)S(1)}, u32[]{:S(2)}, u32[]{:S(2)}) collective-permute-start(s16[64,4224]{1,0:T(8,128)(2,1)} %get-tuple-element.30), channel_id=1, source_target_pairs={{0,32},{32,64},{64,96},{96,128},{128,160},{160,192},{192,224},{224... | collective-permute-start | bytes 1622024 | tf_op jit(solution)/shard_map/ppermute | solution.py:168
  193.1 11.8 %shard_map.50.up_own.down_own.own = f32[512,4096]{1,0:T(8,128)S(1)} custom-call(s32[1]{0:T(128)} %bitcast.1.strip_ref, bf16[1536,4096]{1,0:T(8,128)(2,1)} %all-gather.2.cloned.1.call-done.refs_0_.refs_1_, bf16[1536,4096]{1,0:T(8,128)(2,1)} %all-gather.2.cloned.1.call-done.refs_0_.refs_1_), custom_call_target="tpu_custom_call" | custom-call | flops 6442450944 | bytes 20971520 | tf_op jit(solution)/shard_map/pallas_call | solution.py:47
  204.9 3.3 %copy-done.2 = f32[512,4096]{1,0:T(8,128)} copy-done((f32[512,4096]{1,0:T(8,128)}, f32[512,4096]{1,0:T(8,128)S(1)}, u32[]{:S(2)}) %copy-start.2) | copy-done | bytes 8388632
  208.2 3.7 %shard_map.51 = (s16[32,4224]{1,0:T(8,128)(2,1)}, s16[32,4224]{1,0:T(8,128)(2,1)}) custom-call(s32[2]{0:T(128)} %pad_add_fusion.3.at_ref, f32[512,4096]{1,0:T(8,128)} %copy-done.2, f32[512,4096]{1,0:T(8,128)} %copy-done.2), custom_call_target="tpu_custom_call" | custom-call | flops 2097152 | bytes 2097152 | tf_op jit(solution)/shard_map/pallas_call | solution.py:143
  211.9 3.2 %collective-permute-start.4 = (s16[32,4224]{1,0:T(8,128)(2,1)}, s16[32,4224]{1,0:T(8,128)(2,1)S(1)}, u32[]{:S(2)}, u32[]{:S(2)}) collective-permute-start(s16[32,4224]{1,0:T(8,128)(2,1)} %get-tuple-element.19), channel_id=1, source_target_pairs={{0,224},{32,0},{64,32},{96,64},{128,96},{160,128},{192,160},{224,1... | collective-permute-start | bytes 811016 | tf_op jit(solution)/shard_map/ppermute | solution.py:168
  215.2 4.8 %collective-permute-done.3.up_in = s16[32,4224]{1,0:T(8,128)(2,1)S(1)} collective-permute-done((s16[32,4224]{1,0:T(8,128)(2,1)}, s16[32,4224]{1,0:T(8,128)(2,1)S(1)}, u32[]{:S(2)}, u32[]{:S(2)}) %collective-permute-start.3) | collective-permute-done | bytes 270368 | tf_op jit(solution)/shard_map/ppermute | solution.py:168
  221.4 6.4 %shard_map.52 = (s16[64,4224]{1,0:T(8,128)(2,1)}, s16[64,4224]{1,0:T(8,128)(2,1)}) custom-call(s32[3]{0:T(128)} %pad_add_fusion.2.at_ref, f32[512,4096]{1,0:T(8,128)} %copy-done.2, f32[512,4096]{1,0:T(8,128)} %copy-done.2, s16[32,4224]{1,0:T(8,128)(2,1)} %copy-done.21, s16[32,4224]{1,0:T(8,128)(2,1)} %copy-done.22), custom_call_target="tpu_custom_call" | custom-call | flops 4194304 | bytes 4194304 | tf_op jit(solution)/shard_map/pallas_call | solution.py:143
  227.8 3.2 %collective-permute-start.6 = (s16[64,4224]{1,0:T(8,128)(2,1)}, s16[64,4224]{1,0:T(8,128)(2,1)S(1)}, u32[]{:S(2)}, u32[]{:S(2)}) collective-permute-start(s16[64,4224]{1,0:T(8,128)(2,1)} %get-tuple-element.21), channel_id=1, source_target_pairs={{0,224},{32,0},{64,32},{96,64},{128,96},{160,128},{192,160},{224,1... | collective-permute-start | bytes 1622024 | tf_op jit(solution)/shard_map/ppermute | solution.py:168
  233.2 6.9 %shard_map.60 = (s16[64,4224]{1,0:T(8,128)(2,1)}, s16[64,4224]{1,0:T(8,128)(2,1)}) custom-call(s32[3]{0:T(128)} %pad_add_fusion.1.at_ref, f32[512,4096]{1,0:T(8,128)} %shard_map.56.up_own.down_own.own, f32[512,4096]{1,0:T(8,128)} %shard_map.56.up_own.down_own.own, s16[64,4224]{1,0:T(8,128)(2,1)} %copy-done.7, s16[64,4224]{1,0:T(8,128)(2,1)} %copy-done.8), custom_call_target="tpu_custom_call" | custom-call | flops 4194304 | bytes 4194304 | tf_op jit(solution)/shard_map/pallas_call | solution.py:143
  240.2 3.2 %collective-permute-start.35 = (s16[64,4224]{1,0:T(8,128)(2,1)}, s16[64,4224]{1,0:T(8,128)(2,1)S(1)}, u32[]{:S(2)}, u32[]{:S(2)}) collective-permute-start(s16[64,4224]{1,0:T(8,128)(2,1)} %get-tuple-element.33), channel_id=1, source_target_pairs={{0,224},{32,0},{64,32},{96,64},{128,96},{160,128},{192,160},{224,1... | collective-permute-start | bytes 1622024 | tf_op jit(solution)/shard_map/ppermute | solution.py:184
  245.0 7.0 %shard_map.53 = (s16[64,4224]{1,0:T(8,128)(2,1)}, s16[64,4224]{1,0:T(8,128)(2,1)}) custom-call(s32[3]{0:T(128)} %pad_add_fusion.at_ref, f32[512,4096]{1,0:T(8,128)} %copy-done.2, f32[512,4096]{1,0:T(8,128)} %copy-done.2, s16[64,4224]{1,0:T(8,128)(2,1)} %copy-done.13, s16[64,4224]{1,0:T(8,128)(2,1)} %copy-done.14), custom_call_target="tpu_custom_call" | custom-call | flops 4194304 | bytes 4194304 | tf_op jit(solution)/shard_map/pallas_call | solution.py:143
  256.2 4.1 %shard_map.61 = f32[64,4096]{1,0:T(8,128)} custom-call(s32[1]{0:T(128)} %bitcast.at_ref, f32[1]{0:T(128)} %constant.65.clone.1.scale_ref, f32[512,4096]{1,0:T(8,128)} %shard_map.56.up_own.down_own.own, s16[64,4224]{1,0:T(8,128)(2,1)} %copy-done.15, s16[64,4224]{1,0:T(8,128)(2,1)} %copy-done.16), custom_call_target="tpu_custom_call" | custom-call | flops 4194304 | bytes 3145728 | tf_op jit(solution)/shard_map/pallas_call | solution.py:185
  265.7 7.0 %shard_map.54 = (s16[64,4224]{1,0:T(8,128)(2,1)}, s16[64,4224]{1,0:T(8,128)(2,1)}) custom-call(s32[3]{0:T(128)} %pad_add_fusion.1.at_ref, f32[512,4096]{1,0:T(8,128)} %copy-done.2, f32[512,4096]{1,0:T(8,128)} %copy-done.2, s16[64,4224]{1,0:T(8,128)(2,1)} %copy-done.11, s16[64,4224]{1,0:T(8,128)(2,1)} %copy-done.12), custom_call_target="tpu_custom_call" | custom-call | flops 4194304 | bytes 4194304 | tf_op jit(solution)/shard_map/pallas_call | solution.py:143
  275.9 11.1 %collective-permute-done.36 = f32[64,4096]{1,0:T(8,128)S(1)} collective-permute-done((f32[64,4096]{1,0:T(8,128)}, f32[64,4096]{1,0:T(8,128)S(1)}, u32[]{:S(2)}, u32[]{:S(2)}) %collective-permute-start.36) | collective-permute-done | bytes 1048608 | tf_op jit(solution)/shard_map/ppermute | solution.py:266
  288.6 4.2 %shard_map.55 = f32[64,4096]{1,0:T(8,128)} custom-call(s32[1]{0:T(128)} %bitcast.at_ref, f32[1]{0:T(128)} %constant.65.clone.1.scale_ref, f32[512,4096]{1,0:T(8,128)} %copy-done.2, s16[64,4224]{1,0:T(8,128)(2,1)} %copy-done.17, s16[64,4224]{1,0:T(8,128)(2,1)} %copy-done.18), custom_call_target="tpu_custom_call" | custom-call | flops 4194304 | bytes 3145728 | tf_op jit(solution)/shard_map/pallas_call | solution.py:185
  (148 shorter events, 64.4 us)
Async XLA Ops:
  7.2 185.9 %all-gather.2.cloned.1.call-start = ((), (), s32[]{:S(2)}) async-start(), calls=%async_computation | async-start | bytes 14155776 | tf_op jit(solution)/shard_map/all_gather | solution.py:256
  14.9 13.6 %collective-permute-start.2 = (bf16[48,4096]{1,0:T(8,128)(2,1)S(1)}, bf16[48,4096]{1,0:T(8,128)(2,1)S(1)}, u32[]{:S(2)}, u32[]{:S(2)}) collective-permute-start(bf16[48,4096]{1,0:T(8,128)(2,1)S(1)} %get-tuple-element.39), channel_id=1, source_target_pairs={{0,16},{8,24},{16,0},{24,8},{1,17},{9,25},{17,1},{25,9},{2,18},{10... | collective-permute-start | bytes 1179656 | tf_op jit(solution)/shard_map/ppermute | solution.py:207
  18.2 18.0 %collective-permute-start.1 = (bf16[48,4096]{1,0:T(8,128)(2,1)S(1)}, bf16[48,4096]{1,0:T(8,128)(2,1)S(1)}, u32[]{:S(2)}, u32[]{:S(2)}) collective-permute-start(bf16[48,4096]{1,0:T(8,128)(2,1)S(1)} %get-tuple-element.40), channel_id=1, source_target_pairs={{0,24},{8,0},{16,8},{24,16},{1,25},{9,1},{17,9},{25,17},{2,26},{10... | collective-permute-start | bytes 1179656 | tf_op jit(solution)/shard_map/ppermute | solution.py:207
  19.3 16.9 %collective-permute-start = (bf16[48,4096]{1,0:T(8,128)(2,1)S(1)}, bf16[48,4096]{1,0:T(8,128)(2,1)S(1)}, u32[]{:S(2)}, u32[]{:S(2)}) collective-permute-start(bf16[48,4096]{1,0:T(8,128)(2,1)S(1)} %get-tuple-element.41), channel_id=1, source_target_pairs={{0,8},{8,16},{16,24},{24,0},{1,9},{9,17},{17,25},{25,1},{2,10},{10... | collective-permute-start | bytes 1179656 | tf_op jit(solution)/shard_map/ppermute | solution.py:207
  41.1 12.1 %collective-permute-start.11 = (bf16[48,4096]{1,0:T(8,128)(2,1)S(1)}, bf16[48,4096]{1,0:T(8,128)(2,1)S(1)}, u32[]{:S(2)}, u32[]{:S(2)}) collective-permute-start(bf16[48,4096]{1,0:T(8,128)(2,1)S(1)} %get-tuple-element.36), channel_id=1, source_target_pairs={{0,2},{2,4},{4,6},{6,0},{1,3},{3,5},{5,7},{7,1},{8,10},{10,12},{12... | collective-permute-start | bytes 1179656 | tf_op jit(solution)/shard_map/ppermute | solution.py:207
  42.4 26.3 %collective-permute-start.13 = (bf16[48,4096]{1,0:T(8,128)(2,1)S(1)}, bf16[48,4096]{1,0:T(8,128)(2,1)S(1)}, u32[]{:S(2)}, u32[]{:S(2)}) collective-permute-start(bf16[48,4096]{1,0:T(8,128)(2,1)S(1)} %get-tuple-element.34), channel_id=1, source_target_pairs={{0,4},{2,6},{4,0},{6,2},{1,5},{3,7},{5,1},{7,3},{8,12},{10,14},{12... | collective-permute-start | bytes 1179656 | tf_op jit(solution)/shard_map/ppermute | solution.py:207
  43.2 25.5 %collective-permute-start.12 = (bf16[48,4096]{1,0:T(8,128)(2,1)S(1)}, bf16[48,4096]{1,0:T(8,128)(2,1)S(1)}, u32[]{:S(2)}, u32[]{:S(2)}) collective-permute-start(bf16[48,4096]{1,0:T(8,128)(2,1)S(1)} %get-tuple-element.35), channel_id=1, source_target_pairs={{0,6},{2,0},{4,2},{6,4},{1,7},{3,1},{5,3},{7,5},{8,14},{10,8},{12,... | collective-permute-start | bytes 1179656 | tf_op jit(solution)/shard_map/ppermute | solution.py:207
  53.3 18.5 %collective-permute-start.20 = (bf16[96,4096]{1,0:T(8,128)(2,1)S(1)}, bf16[96,4096]{1,0:T(8,128)(2,1)S(1)}, u32[]{:S(2)}, u32[]{:S(2)}) collective-permute-start(bf16[96,4096]{1,0:T(8,128)(2,1)S(1)} %pad_maximum_fusion.1.refs_0_.refs_16_), channel_id=1, source_target_pairs={{0,1},{1,0},{2,3},{3,2},{4,5},{5,4},{6,7},{7,6},{8,9},{9,8},{10,11... | collective-permute-start | bytes 2359304 | tf_op jit(solution)/shard_map/ppermute | solution.py:223
  53.4 20.5 %collective-permute-start.17 = (bf16[96,4096]{1,0:T(8,128)(2,1)S(1)}, bf16[96,4096]{1,0:T(8,128)(2,1)S(1)}, u32[]{:S(2)}, u32[]{:S(2)}) collective-permute-start(bf16[96,4096]{1,0:T(8,128)(2,1)S(1)} %pad_maximum_fusion.1.refs_0_.refs_16_), channel_id=1, source_target_pairs={{0,24},{8,0},{16,8},{24,16},{1,25},{9,1},{17,9},{25,17},{2,26},{10... | collective-permute-start | bytes 2359304 | tf_op jit(solution)/shard_map/ppermute | solution.py:219
  56.0 21.4 %collective-permute-start.14 = (bf16[96,4096]{1,0:T(8,128)(2,1)S(1)}, bf16[96,4096]{1,0:T(8,128)(2,1)}, u32[]{:S(2)}, u32[]{:S(2)}) collective-permute-start(bf16[96,4096]{1,0:T(8,128)(2,1)S(1)} %pad_maximum_fusion.1.refs_0_.refs_16_), channel_id=1, source_target_pairs={{0,8},{8,16},{16,24},{24,0},{1,9},{9,17},{17,25},{25,1},{2,10},{10... | collective-permute-start | bytes 2359304 | tf_op jit(solution)/shard_map/ppermute | solution.py:216
  68.7 21.6 %collective-permute-start.15 = (bf16[96,4096]{1,0:T(8,128)(2,1)S(1)}, bf16[96,4096]{1,0:T(8,128)(2,1)}, u32[]{:S(2)}, u32[]{:S(2)}) collective-permute-start(bf16[96,4096]{1,0:T(8,128)(2,1)S(1)} %constant_dynamic-update-slice_fusion.refs_1_.refs_17_), channel_id=1, source_target_pairs={{0,24},{8,0},{16,8},{24,16},{1,25},{9,1},{17,9},{25,17},{2,26},{10... | collective-permute-start | bytes 2359304 | tf_op jit(solution)/shard_map/ppermute | solution.py:217
  71.7 22.3 %collective-permute-start.21 = (bf16[96,4096]{1,0:T(8,128)(2,1)S(1)}, bf16[96,4096]{1,0:T(8,128)(2,1)S(1)}, u32[]{:S(2)}, u32[]{:S(2)}) collective-permute-start(bf16[96,4096]{1,0:T(8,128)(2,1)S(1)} %constant_dynamic-update-slice_fusion.refs_1_.refs_17_), channel_id=1, source_target_pairs={{0,1},{1,0},{2,3},{3,2},{4,5},{5,4},{6,7},{7,6},{8,9},{9,8},{10,11... | collective-permute-start | bytes 2359304 | tf_op jit(solution)/shard_map/ppermute | solution.py:223
  71.7 23.2 %collective-permute-start.16 = (bf16[96,4096]{1,0:T(8,128)(2,1)S(1)}, bf16[96,4096]{1,0:T(8,128)(2,1)}, u32[]{:S(2)}, u32[]{:S(2)}) collective-permute-start(bf16[96,4096]{1,0:T(8,128)(2,1)S(1)} %constant_dynamic-update-slice_fusion.refs_1_.refs_17_), channel_id=1, source_target_pairs={{0,8},{8,16},{16,24},{24,0},{1,9},{9,17},{17,25},{25,1},{2,10},{10... | collective-permute-start | bytes 2359304 | tf_op jit(solution)/shard_map/ppermute | solution.py:218
  73.9 21.6 %collective-permute-start.25 = (bf16[96,4096]{1,0:T(8,128)(2,1)S(1)}, bf16[96,4096]{1,0:T(8,128)(2,1)S(1)}, u32[]{:S(2)}, u32[]{:S(2)}) collective-permute-start(bf16[96,4096]{1,0:T(8,128)(2,1)S(1)} %collective-permute-done.17.refs_5_.refs_21_), channel_id=1, source_target_pairs={{0,1},{1,0},{2,3},{3,2},{4,5},{5,4},{6,7},{7,6},{8,9},{9,8},{10,11... | collective-permute-start | bytes 2359304 | tf_op jit(solution)/shard_map/ppermute | solution.py:223
  77.4 33.3 %collective-permute-start.18 = (bf16[96,4096]{1,0:T(8,128)(2,1)}, bf16[96,4096]{1,0:T(8,128)(2,1)}, u32[]{:S(2)}, u32[]{:S(2)}) collective-permute-start(bf16[96,4096]{1,0:T(8,128)(2,1)} %collective-permute-done.14.refs_2_.refs_18_), channel_id=1, source_target_pairs={{0,8},{8,16},{16,24},{24,0},{1,9},{9,17},{17,25},{25,1},{2,10},{10... | collective-permute-start | bytes 2359304 | tf_op jit(solution)/shard_map/ppermute | solution.py:220
  90.3 20.7 %collective-permute-start.19 = (bf16[96,4096]{1,0:T(8,128)(2,1)}, bf16[96,4096]{1,0:T(8,128)(2,1)}, u32[]{:S(2)}, u32[]{:S(2)}) collective-permute-start(bf16[96,4096]{1,0:T(8,128)(2,1)} %collective-permute-done.15.refs_3_.refs_19_), channel_id=1, source_target_pairs={{0,24},{8,0},{16,8},{24,16},{1,25},{9,1},{17,9},{25,17},{2,26},{10... | collective-permute-start | bytes 2359304 | tf_op jit(solution)/shard_map/ppermute | solution.py:221
  94.9 16.8 %collective-permute-start.22 = (bf16[96,4096]{1,0:T(8,128)(2,1)}, bf16[96,4096]{1,0:T(8,128)(2,1)}, u32[]{:S(2)}, u32[]{:S(2)}) collective-permute-start(bf16[96,4096]{1,0:T(8,128)(2,1)} %collective-permute-done.14.refs_2_.refs_18_), channel_id=1, source_target_pairs={{0,1},{1,0},{2,3},{3,2},{4,5},{5,4},{6,7},{7,6},{8,9},{9,8},{10,11... | collective-permute-start | bytes 2359304 | tf_op jit(solution)/shard_map/ppermute | solution.py:223
  94.9 16.8 %collective-permute-start.23 = (bf16[96,4096]{1,0:T(8,128)(2,1)}, bf16[96,4096]{1,0:T(8,128)(2,1)}, u32[]{:S(2)}, u32[]{:S(2)}) collective-permute-start(bf16[96,4096]{1,0:T(8,128)(2,1)} %collective-permute-done.15.refs_3_.refs_19_), channel_id=1, source_target_pairs={{0,1},{1,0},{2,3},{3,2},{4,5},{5,4},{6,7},{7,6},{8,9},{9,8},{10,11... | collective-permute-start | bytes 2359304 | tf_op jit(solution)/shard_map/ppermute | solution.py:223
  96.3 15.4 %collective-permute-start.24 = (bf16[96,4096]{1,0:T(8,128)(2,1)}, bf16[96,4096]{1,0:T(8,128)(2,1)}, u32[]{:S(2)}, u32[]{:S(2)}) collective-permute-start(bf16[96,4096]{1,0:T(8,128)(2,1)} %collective-permute-done.16.refs_4_.refs_20_), channel_id=1, source_target_pairs={{0,1},{1,0},{2,3},{3,2},{4,5},{5,4},{6,7},{7,6},{8,9},{9,8},{10,11... | collective-permute-start | bytes 2359304 | tf_op jit(solution)/shard_map/ppermute | solution.py:223
  133.8 14.8 %collective-permute-start.28 = (s16[32,4224]{1,0:T(8,128)(2,1)}, s16[32,4224]{1,0:T(8,128)(2,1)S(1)}, u32[]{:S(2)}, u32[]{:S(2)}) collective-permute-start(s16[32,4224]{1,0:T(8,128)(2,1)} %get-tuple-element.26), channel_id=1, source_target_pairs={{0,32},{32,64},{64,96},{96,128},{128,160},{160,192},{192,224},{224... | collective-permute-start | bytes 811016 | tf_op jit(solution)/shard_map/ppermute | solution.py:168
  135.7 12.9 %collective-permute-start.29 = (s16[32,4224]{1,0:T(8,128)(2,1)}, s16[32,4224]{1,0:T(8,128)(2,1)S(1)}, u32[]{:S(2)}, u32[]{:S(2)}) collective-permute-start(s16[32,4224]{1,0:T(8,128)(2,1)} %get-tuple-element.27), channel_id=1, source_target_pairs={{0,224},{32,0},{64,32},{96,64},{128,96},{160,128},{192,160},{224,1... | collective-permute-start | bytes 811016 | tf_op jit(solution)/shard_map/ppermute | solution.py:168
  156.4 15.2 %collective-permute-start.30 = (s16[64,4224]{1,0:T(8,128)(2,1)}, s16[64,4224]{1,0:T(8,128)(2,1)S(1)}, u32[]{:S(2)}, u32[]{:S(2)}) collective-permute-start(s16[64,4224]{1,0:T(8,128)(2,1)} %get-tuple-element.28), channel_id=1, source_target_pairs={{0,32},{32,64},{64,96},{96,128},{128,160},{160,192},{192,224},{224... | collective-permute-start | bytes 1622024 | tf_op jit(solution)/shard_map/ppermute | solution.py:168
  156.4 15.2 %collective-permute-start.31 = (s16[64,4224]{1,0:T(8,128)(2,1)}, s16[64,4224]{1,0:T(8,128)(2,1)S(1)}, u32[]{:S(2)}, u32[]{:S(2)}) collective-permute-start(s16[64,4224]{1,0:T(8,128)(2,1)} %get-tuple-element.29), channel_id=1, source_target_pairs={{0,224},{32,0},{64,32},{96,64},{128,96},{160,128},{192,160},{224,1... | collective-permute-start | bytes 1622024 | tf_op jit(solution)/shard_map/ppermute | solution.py:168
  180.2 51.5 %collective-permute-start.32 = (s16[64,4224]{1,0:T(8,128)(2,1)}, s16[64,4224]{1,0:T(8,128)(2,1)S(1)}, u32[]{:S(2)}, u32[]{:S(2)}) collective-permute-start(s16[64,4224]{1,0:T(8,128)(2,1)} %get-tuple-element.30), channel_id=1, source_target_pairs={{0,32},{32,64},{64,96},{96,128},{128,160},{160,192},{192,224},{224... | collective-permute-start | bytes 1622024 | tf_op jit(solution)/shard_map/ppermute | solution.py:168
  189.8 41.8 %collective-permute-start.33 = (s16[64,4224]{1,0:T(8,128)(2,1)}, s16[64,4224]{1,0:T(8,128)(2,1)S(1)}, u32[]{:S(2)}, u32[]{:S(2)}) collective-permute-start(s16[64,4224]{1,0:T(8,128)(2,1)} %get-tuple-element.31), channel_id=1, source_target_pairs={{0,224},{32,0},{64,32},{96,64},{128,96},{160,128},{192,160},{224,1... | collective-permute-start | bytes 1622024 | tf_op jit(solution)/shard_map/ppermute | solution.py:168
  227.8 15.7 %collective-permute-start.5 = (s16[64,4224]{1,0:T(8,128)(2,1)}, s16[64,4224]{1,0:T(8,128)(2,1)S(1)}, u32[]{:S(2)}, u32[]{:S(2)}) collective-permute-start(s16[64,4224]{1,0:T(8,128)(2,1)} %get-tuple-element.20), channel_id=1, source_target_pairs={{0,32},{32,64},{64,96},{96,128},{128,160},{160,192},{192,224},{224... | collective-permute-start | bytes 1622024 | tf_op jit(solution)/shard_map/ppermute | solution.py:168
  227.8 15.7 %collective-permute-start.6 = (s16[64,4224]{1,0:T(8,128)(2,1)}, s16[64,4224]{1,0:T(8,128)(2,1)S(1)}, u32[]{:S(2)}, u32[]{:S(2)}) collective-permute-start(s16[64,4224]{1,0:T(8,128)(2,1)} %get-tuple-element.21), channel_id=1, source_target_pairs={{0,224},{32,0},{64,32},{96,64},{128,96},{160,128},{192,160},{224,1... | collective-permute-start | bytes 1622024 | tf_op jit(solution)/shard_map/ppermute | solution.py:168
  240.2 15.0 %collective-permute-start.34 = (s16[64,4224]{1,0:T(8,128)(2,1)}, s16[64,4224]{1,0:T(8,128)(2,1)S(1)}, u32[]{:S(2)}, u32[]{:S(2)}) collective-permute-start(s16[64,4224]{1,0:T(8,128)(2,1)} %get-tuple-element.32), channel_id=1, source_target_pairs={{0,32},{32,64},{64,96},{96,128},{128,160},{160,192},{192,224},{224... | collective-permute-start | bytes 1622024 | tf_op jit(solution)/shard_map/ppermute | solution.py:184
  240.2 15.0 %collective-permute-start.35 = (s16[64,4224]{1,0:T(8,128)(2,1)}, s16[64,4224]{1,0:T(8,128)(2,1)S(1)}, u32[]{:S(2)}, u32[]{:S(2)}) collective-permute-start(s16[64,4224]{1,0:T(8,128)(2,1)} %get-tuple-element.33), channel_id=1, source_target_pairs={{0,224},{32,0},{64,32},{96,64},{128,96},{160,128},{192,160},{224,1... | collective-permute-start | bytes 1622024 | tf_op jit(solution)/shard_map/ppermute | solution.py:184
  260.3 26.6 %collective-permute-start.36 = (f32[64,4096]{1,0:T(8,128)}, f32[64,4096]{1,0:T(8,128)S(1)}, u32[]{:S(2)}, u32[]{:S(2)}) collective-permute-start(f32[64,4096]{1,0:T(8,128)} %shard_map.61), channel_id=1, source_target_pairs={{0,0},{2,10},{4,20},{6,30},{8,2},{10,12},{12,22},{14,24},{16,4},{1... | collective-permute-start | bytes 3145736 | tf_op jit(solution)/shard_map/ppermute | solution.py:266
  272.6 14.4 %collective-permute-start.9 = (s16[64,4224]{1,0:T(8,128)(2,1)}, s16[64,4224]{1,0:T(8,128)(2,1)S(1)}, u32[]{:S(2)}, u32[]{:S(2)}) collective-permute-start(s16[64,4224]{1,0:T(8,128)(2,1)} %get-tuple-element.24), channel_id=1, source_target_pairs={{0,32},{32,64},{64,96},{96,128},{128,160},{160,192},{192,224},{224... | collective-permute-start | bytes 1622024 | tf_op jit(solution)/shard_map/ppermute | solution.py:184
  272.6 14.4 %collective-permute-start.10 = (s16[64,4224]{1,0:T(8,128)(2,1)}, s16[64,4224]{1,0:T(8,128)(2,1)S(1)}, u32[]{:S(2)}, u32[]{:S(2)}) collective-permute-start(s16[64,4224]{1,0:T(8,128)(2,1)} %get-tuple-element.25), channel_id=1, source_target_pairs={{0,224},{32,0},{64,32},{96,64},{128,96},{160,128},{192,160},{224,1... | collective-permute-start | bytes 1622024 | tf_op jit(solution)/shard_map/ppermute | solution.py:184
  (29 other events, 78.6 us)
Sparse Core Ops, SparseCore 0:
  37.6 77.0 all-gather.1
